TPU v7x, 512 devices: a whole 4x4x16 slice. The times are simulated.
512 devices in a mesh: member: 64 (over z, y_hi, core), tensor: 8 (over y_lo, x).
Axes of the slice: x: 4, y: 4 (y_hi: 2, y_lo: 2; y = y_hi * 2 + y_lo), z: 16, core: 2. Of those that a mesh axis runs over, the one named last changes fastest.
Arguments:
- inputs: bfloat16 [1024, 5120], P('member', 'tensor'), may hold values from -6 to 6
- key_weight: bfloat16 [5120, 20480], P('tensor', 'member'), may hold values from -0.078125 to 0.078125
- value_weight: bfloat16 [20480, 5120], P('member', 'tensor'), may hold values from -0.0390625 to 0.0390625
- key_probe: bfloat16 [1024, 5120], P('member', 'tensor'), may hold values from -6 to 6
- key_spread: bfloat16 [1024, 20480], P('tensor', 'member'), may hold values from -6 to 6
- value_probe: bfloat16 [1024, 20480], P('tensor', 'member'), may hold values from -6 to 6
- value_spread: bfloat16 [1024, 5120], P('member', 'tensor'), may hold values from -6 to 6
- fitness: bfloat16 [1024], P('member'), may hold values from -6 to 6
Outputs:
- outputs: bfloat16 [1024, 5120], P('member', 'tensor')
- key_update: bfloat16 [5120, 20480], P('tensor', 'member')
- value_update: bfloat16 [20480, 5120], P('member', 'tensor')
All inputs are finite; a program needn't handle non-finite values.
Results may differ from a plain program's by a relative error of at most 0.0065.
Values may be sent and summed in bfloat16 or wider, within the bound.
A program may use at most 64 MiB of HBM per device.

v0:
```python
import math

import jax
import jax.numpy as jnp
from jax import lax
from jax.sharding import PartitionSpec as P

sigma_scale = 0.005


def row_dots(left, right):
    return jnp.sum(left.astype(jnp.float32) * right.astype(jnp.float32), axis=1)


def outer_sum(probe_rows, spread_rows, fitness_rows):
    factor = fitness_rows.astype(jnp.float32)[:, None] * (1.0 / math.sqrt(probe_rows.shape[0]))
    weighted = (factor * spread_rows.astype(jnp.float32)).astype(jnp.bfloat16)
    summed = lax.dot_general(
        probe_rows, weighted, (((0,), (0,)), ((), ())), preferred_element_type=jnp.float32
    )
    return summed.astype(jnp.bfloat16)


def body(
    inputs, key_weight, value_weight, key_probe, key_spread, value_probe, value_spread, fitness
):
    input_all, probe_all, spread_all, fitness_all = (
        lax.all_gather(inputs, "member", axis=0, tiled=True),
        lax.all_gather(key_probe, "member", axis=0, tiled=True),
        lax.all_gather(value_spread, "member", axis=0, tiled=True),
        lax.all_gather(fitness, "member", axis=0, tiled=True),
    )
    key_partial = jnp.dot(input_all, key_weight, preferred_element_type=jnp.float32)
    key_dots_partial = row_dots(input_all, probe_all)
    key_part, key_dots = (
        lax.psum_scatter(key_partial, "tensor", scatter_dimension=0, tiled=True),
        lax.psum_scatter(key_dots_partial, "tensor", scatter_dimension=0, tiled=True),
    )
    key_pre = key_part + sigma_scale * key_dots[:, None] * key_spread.astype(jnp.float32)
    hidden = (jnp.maximum(key_pre, 0.0) ** 2).astype(jnp.bfloat16)
    hidden_all, vprobe_all, kspread_all = (
        lax.all_gather(hidden, "tensor", axis=0, tiled=True),
        lax.all_gather(value_probe, "tensor", axis=0, tiled=True),
        lax.all_gather(key_spread, "tensor", axis=0, tiled=True),
    )
    value_partial = jnp.dot(hidden_all, value_weight, preferred_element_type=jnp.float32)
    value_dots_partial = row_dots(hidden_all, vprobe_all)
    value_part, value_dots = (
        lax.psum_scatter(value_partial, "member", scatter_dimension=0, tiled=True),
        lax.psum_scatter(value_dots_partial, "member", scatter_dimension=0, tiled=True),
    )
    outputs = (
        value_part + sigma_scale * value_dots[:, None] * value_spread.astype(jnp.float32)
    ).astype(jnp.bfloat16)
    key_update = outer_sum(probe_all, kspread_all, fitness_all)
    value_update = outer_sum(vprobe_all, spread_all, fitness_all)
    return (outputs, key_update, value_update)


def solution(mesh):
    placed = (
        P("member", "tensor"),
        P("tensor", "member"),
        P("member", "tensor"),
        P("member", "tensor"),
        P("tensor", "member"),
        P("tensor", "member"),
        P("member", "tensor"),
        P("member"),
    )
    return jax.shard_map(
        body,
        mesh=mesh,
        in_specs=placed,
        out_specs=(P("member", "tensor"), P("tensor", "member"), P("member", "tensor")),
        check_vma=False,
    )
```

profile of v0, /device:TPU:4, one launch (start us, length us, event | category | flops | bytes accessed | tf_op | source)
XLA Modules:
  0.0 708.1 jit_solution(5656730598569791111)
XLA Ops:
  7.2 0.0 all-gather.4.cloned.1.call-start
  7.2 0.7 all-gather.4.cloned.1.call-update
  7.9 0.0 all-gather.6.cloned.1.call-start
  8.0 0.7 all-gather.6.cloned.1.call-update
  8.7 0.0 reduce-scatter.3.cloned.1.call-start
  8.7 148.0 %all-gather.4.cloned.1.call-done = bf16[1024,640]{1,0:T(8,128)(2,1)} async-done(((bf16[16,640]{1,0:T(8,128)(2,1)}), bf16[1024,640]{1,0:T(8,128)(2,1)}) %all-gather.4.cloned.1.call-update) | async-done | bytes 1310736 | tf_op jit(solution)/shard_map/all_gather | solution.py:28
  156.7 3.2 fusion.7
  159.9 0.0 all-gather.8.cloned.1.call-start
  160.0 0.5 all-gather.8.cloned.1.call-update
  160.5 0.0 reduce-scatter.5.cloned.1.call-start
  160.5 1.3 dynamic-slice.1
  162.5 133.3 %all-gather.6.cloned.1.call-done = bf16[1024,640]{1,0:T(8,128)(2,1)} async-done(((bf16[16,640]{1,0:T(8,128)(2,1)}), bf16[1024,640]{1,0:T(8,128)(2,1)}) %all-gather.6.cloned.1.call-update) | async-done | bytes 1310736 | tf_op jit(solution)/shard_map/all_gather | solution.py:29
  295.8 1.7 multiply_reduce_fusion
  297.5 15.6 %all-reduce.1 = f32[1024]{0:T(1024)S(1)} all-reduce(f32[1024]{0:T(1024)S(1)} %multiply_reduce_fusion), channel_id=3, replica_groups=mesh['member'=64,'tensor'=8] {'tensor'}, use_global_device_ids=true, to_apply=%region_2.0.clone | all-reduce | flops 1024 | bytes 8192
  313.1 0.1 dynamic-slice_multiply_fusion.1
  313.2 25.3 %reduce-scatter.3.cloned.1.call-done = f32[128,320]{0,1:T(8,128)} async-done(((f32[1024,320]{0,1:T(8,128)}), f32[128,320]{0,1:T(8,128)}) %reduce-scatter.3.cloned.1.call-update) | async-done | bytes 163856 | tf_op jit(solution)/shard_map/reduce_scatter | solution.py:36
  338.5 1.0 multiply_convert_fusion.8
  339.5 27.0 %all_gather.23 = bf16[1024,320]{0,1:T(8,128)(2,1)S(1)} all-gather(bf16[128,320]{0,1:T(8,128)(2,1)S(1)} %multiply_convert_fusion.8), channel_id=1, replica_groups=mesh['member'=64,'tensor'=8] {'tensor'}, dimensions={0}, use_global_device_ids=true | all-gather | bytes 737280 | tf_op jit(solution)/shard_map/all_gather | solution.py:42
  366.5 2.5 fusion.8
  369.0 0.6 copy-done.6
  369.6 0.6 fusion.6
  371.6 0.2 dynamic-update-slice
  371.8 129.4 %all-reduce = bf16[1024]{0:T(1024)(128)(2,1)S(1)} all-reduce(bf16[1024]{0:T(1024)(128)(2,1)S(1)} %dynamic-update-slice), channel_id=1, replica_groups=mesh['member'=64,'tensor'=8] {'member'}, use_global_device_ids=true, to_apply=%add | all-reduce | flops 1024 | bytes 4096
  501.2 26.2 %all_gather.26 = bf16[1024,320]{0,1:T(8,128)(2,1)S(1)} all-gather(bf16[128,320]{0,1:T(8,128)(2,1)S(1)} %copy-done.3), channel_id=1, replica_groups=mesh['member'=64,'tensor'=8] {'tensor'}, dimensions={0}, use_global_device_ids=true | all-gather | bytes 737280 | tf_op jit(solution)/shard_map/all_gather | solution.py:44
  527.4 26.4 %all_gather.24 = bf16[1024,320]{0,1:T(8,128)(2,1)S(1)} all-gather(bf16[128,320]{0,1:T(8,128)(2,1)S(1)} %copy-done.5), channel_id=1, replica_groups=mesh['member'=64,'tensor'=8] {'tensor'}, dimensions={0}, use_global_device_ids=true | all-gather | bytes 737280 | tf_op jit(solution)/shard_map/all_gather | solution.py:43
  553.8 1.4 fusion.3
  555.2 2.9 fusion.4
  558.1 0.3 multiply_reduce_fusion.1
  558.3 129.1 %all-reduce.2 = f32[1024]{0:T(1024)S(1)} all-reduce(f32[1024]{0:T(1024)S(1)} %multiply_reduce_fusion.1), channel_id=5, replica_groups=mesh['member'=64,'tensor'=8] {'member'}, use_global_device_ids=true, to_apply=%region_5.0.clone | all-reduce | flops 1024 | bytes 8192
  687.4 0.1 dynamic-slice_multiply_fusion
  687.5 12.6 %reduce-scatter.5.cloned.1.call-done = f32[16,640]{1,0:T(8,128)} async-done(((f32[1024,640]{1,0:T(8,128)}), f32[16,640]{1,0:T(8,128)}) %reduce-scatter.5.cloned.1.call-update) | async-done | bytes 40976 | tf_op jit(solution)/shard_map/reduce_scatter | solution.py:49
  700.1 1.5 add_convert_fusion
  (20 shorter events, 0.1 us)
Async XLA Ops:
  7.2 359.3 %copy-start = (bf16[320,640]{1,0:T(8,128)(2,1)S(1)}, bf16[320,640]{1,0:T(8,128)(2,1)}, u32[]{:S(2)}) copy-start(bf16[320,640]{1,0:T(8,128)(2,1)} %param.10) | copy-start | bytes 1228804
  7.2 149.5 %all-gather.4.cloned.1.call-start = ((), (), s32[]{:S(2)}) async-start(), calls=%async_computation.2 | async-start | bytes 1331200 | tf_op jit(solution)/shard_map/all_gather | solution.py:28
  7.9 287.9 %all-gather.6.cloned.1.call-start = ((), (), s32[]{:S(2)}) async-start(), calls=%async_computation.4 | async-start | bytes 1331200 | tf_op jit(solution)/shard_map/all_gather | solution.py:29
  8.7 329.9 %reduce-scatter.3.cloned.1.call-start = ((), (), s32[]{:S(2)}) async-start(), calls=%async_computation.3 | async-start | bytes 1474560 | tf_op jit(solution)/shard_map/reduce_scatter | solution.py:36
  159.9 135.9 %copy-start.1 = (bf16[1024,640]{1,0:T(8,128)(2,1)S(1)}, bf16[1024,640]{1,0:T(8,128)(2,1)}, u32[]{:S(2)}) copy-start(bf16[1024,640]{1,0:T(8,128)(2,1)} %all-gather.4.cloned.1.call-done) | copy-start | bytes 3932164
  159.9 395.3 %all-gather.8.cloned.1.call-start = ((), (), s32[]{:S(2)}) async-start(), calls=%async_computation.6 | async-start | bytes 1331200 | tf_op jit(solution)/shard_map/all_gather | solution.py:30
  160.5 539.6 %reduce-scatter.5.cloned.1.call-start = ((), (), s32[]{:S(2)}) async-start(), calls=%async_computation.5 | async-start | bytes 2662400 | tf_op jit(solution)/shard_map/reduce_scatter | solution.py:49
  162.5 176.1 %copy-start.3 = (bf16[128,320]{0,1:T(8,128)(2,1)S(1)}, bf16[128,320]{0,1:T(8,128)(2,1)}, u32[]{:S(2)}) copy-start(bf16[128,320]{0,1:T(8,128)(2,1)} %param.12) | copy-start | bytes 245764
  369.0 0.7 copy-start.6
  369.0 2.6 copy-start.7
  369.0 158.4 %copy-start.5 = (bf16[128,320]{0,1:T(8,128)(2,1)S(1)}, bf16[128,320]{0,1:T(8,128)(2,1)}, u32[]{:S(2)}) copy-start(bf16[128,320]{0,1:T(8,128)(2,1)} %param.13) | copy-start | bytes 245764
  369.0 184.8 %copy-start.2 = (bf16[1024,640]{1,0:T(8,128)(2,1)S(1)}, bf16[1024,640]{1,0:T(8,128)(2,1)}, u32[]{:S(2)}) copy-start(bf16[1024,640]{1,0:T(8,128)(2,1)} %all-gather.6.cloned.1.call-done) | copy-start | bytes 3932164
  558.1 142.0 %copy-start.4 = (bf16[16,640]{1,0:T(8,128)(2,1)S(1)}, bf16[16,640]{1,0:T(8,128)(2,1)}, u32[]{:S(2)}) copy-start(bf16[16,640]{1,0:T(8,128)(2,1)} %param.14) | copy-start | bytes 61444
Sparse Core Ops, SparseCore 0:
  11.2 145.4 all-gather.3
  159.9 135.8 all-gather.5
  298.6 39.8 reduce-scatter.2
  341.6 142.3 all-gather.7
  488.5 211.5 reduce-scatter.4
where the time goes:
time: 708 us
  blocking collectives  354 us (50%)
  waiting for transfers between devices  321 us (45%)
  between operations  15.8 us (2%)
  matrix products  9.93 us (1%)
    unnamed x3, blocking collectives  274 us
    all_gather x1, waiting for transfers between devices, body(): lax.all_gather(inputs, 'member', axis=0, tiled=True)  148 us
    all_gather x1, waiting for transfers between devices, body(): lax.all_gather(key_probe, 'member', axis=0, tiled=True)  133 us
    all_gather x1, blocking collectives, body(): lax.all_gather(hidden, 'tensor', axis=0, tiled=True)  27 us
    all_gather x1, blocking collectives, body(): lax.all_gather(value_probe, 'tensor', axis=0, tiled=True)  26.4 us
    all_gather x1, blocking collectives, body(): lax.all_gather(key_spread, 'tensor', axis=0, tiled=True)  26.2 us
    reduce_scatter x1, waiting for transfers between devices, body(): lax.psum_scatter(key_partial, 'tensor', scatter_dimension=0, tiled=True)  25.3 us
  transfers between devices with their start and end apart: 5, of which 4 were waited for; matrix products, arithmetic and copies ran while one was open for 2% of the time, Pallas kernels for 0%

commit v1 on v0

v1 whole, which is shorter than its diff:
```python
import functools

import jax
import jax.numpy as jnp
from jax import lax
from jax.experimental import pallas as pl
from jax.experimental.pallas import tpu as pltpu
from jax.sharding import PartitionSpec as P

BF, F32 = jnp.bfloat16, jnp.float32
MESH = pl.DeviceIdType.MESH
SIGMA = 0.005

FAR = (4, -4, 8)
NEAR = (
    (1, 0), (-1, 0), (2, 0), (-2, 0),
    (1, -4), (-1, -4), (2, -4),
    (1, 4), (-1, 4), (-2, 4),
    (1, 8), (-1, 8),
)
OFFSETS = (0, -1, 1, -2, 2, -4, 4, -5, 3, -3, 5, -6, 6, 8, 7, -7)


def kernel(
    x_ref, kw_ref, vw_ref, kp_ref, ks_ref, vp_ref, vs_ref, f_ref,
    out_ref, ku_ref, vu_ref,
    gi, gr, ksa, vpa, bsend, rsb, hid, wgt_k, wgt_v, pbuf, psend, rsib, ysend, ry, zf, zb, rn, rn2, fb, rf,
    zs, zr, ys, yr, cs, cr, zs2, zr2, ys2, yr2, cs2, cr2, ts, tr, s_core, r_core, s_y, r_y, s_z, r_z, s_f, r_f,
):
    m, t = lax.axis_index("member"), lax.axis_index("tensor")
    z, half, core = m // 4, (m // 2) % 2, m % 2
    other, sib = 1 - half, 1 - core

    def at_z(dz):
        return (lax.rem(z + dz + 16, 16) * 4 + half * 2 + core, t)

    y_dev = (z * 4 + other * 2 + core, t)
    c_dev = (z * 4 + half * 2 + sib, t)

    def tau(tt):
        return lax.rem(tt, 2) * 4 + tt // 2

    def slot(dz):
        zz = lax.rem(z + dz + 16, 16)
        return (lax.rem(zz, 4) // 2) * 4 + zz // 4, lax.rem(zz, 2)

    def klass(r):
        cc = lax.rem(z + r, 4)
        return pl.ds((cc // 2) * 4, 4), lax.rem(cc, 2)

    me_tau = tau(t)
    pending = []

    def copy(src, dst, ssem, rsem, dev):
        return pltpu.make_async_remote_copy(
            src_ref=src, dst_ref=dst, send_sem=ssem, recv_sem=rsem, device_id=dev, device_id_type=MESH
        )

    def send(src, dst, ssem, rsem, dev):
        c = copy(src, dst, ssem, rsem, dev)
        c.start()
        pending.append(c)

    def arrive(dst, ssem, rsem, dev):
        copy(dst, dst, ssem, rsem, dev).wait_recv()

    bar = pltpu.get_barrier_semaphore()
    partners = [at_z(d) for d in (1, -1, 2, -2, 4, -4, 8)] + [y_dev, c_dev]
    partners += [(m, lax.rem(t + k, 8)) for k in range(1, 8)]
    for dev in partners:
        pl.semaphore_signal(bar, inc=1, device_id=dev, device_id_type=MESH)

    fit = jnp.broadcast_to(f_ref[...].astype(F32), (16, 16))
    row, lane = (lax.broadcasted_iota(jnp.int32, (16, 16), d) for d in (0, 1))
    fit = jnp.sum(jnp.where(row == lane, fit, 0.0), axis=1, keepdims=True)
    dots = jnp.sum(x_ref[...].astype(F32) * kp_ref[...].astype(F32), axis=1, keepdims=True)
    high = dots.astype(BF).astype(F32)
    lanes = lax.broadcasted_iota(jnp.int32, (16, 128), 1)
    aux = jnp.where(lanes == 0, high, jnp.where(lanes == 1, dots - high, jnp.where(lanes == 2, fit, 0.0)))
    st, sl = slot(0)
    gi[st, sl, half, core, :, 0:640] = x_ref[...]
    gi[st, sl, half, core, :, 640:768] = aux.astype(BF)
    gr[st, sl, half, core, :, 0:640] = kp_ref[...]
    gr[st, sl, half, core, :, 640:1280] = vs_ref[...]
    ksa[me_tau] = ks_ref[...]
    vpa[me_tau] = vp_ref[...]

    pl.semaphore_wait(bar, len(partners))

    def chunk(g, dz, hh=None, cc=None):
        a, b = slot(dz)
        return g.at[a, b, half if hh is None else hh, core if cc is None else cc]

    def block(g, r, hh, cc):
        a, b = klass(r)
        return g.at[a, b, hh, cc]

    def far_send(g, s, r):
        for k, d in enumerate(FAR):
            send(chunk(g, 0), chunk(g, 0), s.at[k], r.at[k], at_z(d))

    def near_send(g, s, r, o):
        for k, (d, oo) in enumerate(NEAR):
            if oo == o:
                send(chunk(g, o), chunk(g, o), s.at[3 + k], r.at[3 + k], at_z(d))

    def far_wait(g, s, r, k):
        arrive(chunk(g, -FAR[k]), s.at[k], r.at[k], at_z(-FAR[k]))

    def near_wait(g, s, r, o, then=None):
        for k, (d, oo) in enumerate(NEAR):
            if oo == o:
                arrive(chunk(g, oo - d), s.at[3 + k], r.at[3 + k], at_z(-d))
                if then is not None:
                    then(oo - d)

    def y_send(dz):
        dz = dz if dz <= 8 else dz - 16
        k = OFFSETS.index(dz)
        send(chunk(gi, dz), chunk(gi, dz), ys.at[k], yr.at[k], y_dev)

    far_send(gi, zs, zr)
    near_send(gi, zs, zr, 0)
    y_send(0)
    far_send(gr, zs2, zr2)
    near_send(gr, zs2, zr2, 0)

    def spread(buf, base):
        for k in range(1, 8):
            dev = (m, lax.rem(t + k, 8))
            send(buf.at[me_tau], buf.at[me_tau], ts.at[base + k], tr.at[base + k], dev)

    def spread_wait(buf, base):
        for k in range(1, 8):
            frm = lax.rem(t + 8 - k, 8)
            arrive(buf.at[tau(frm)], ts.at[base + k], tr.at[base + k], (m, frm))

    spread(ksa, 0)

    near_wait(gi, zs, zr, 0, y_send)
    for k, o in ((0, -4), (1, 4)):
        far_wait(gi, zs, zr, k)
        near_send(gi, zs, zr, o)
        y_send(o)
    near_wait(gi, zs, zr, -4, y_send)
    near_wait(gi, zs, zr, 4, y_send)
    far_wait(gi, zs, zr, 2)
    near_send(gi, zs, zr, 8)
    y_send(8)
    near_wait(gi, zs, zr, 8, y_send)
    for r in range(4):
        send(block(gi, r, half, core), block(gi, r, half, core), cs.at[r], cr.at[r], c_dev)
    near_wait(gr, zs2, zr2, 0)
    for k, o in ((0, -4), (1, 4), (2, 8)):
        far_wait(gr, zs2, zr2, k)
        near_send(gr, zs2, zr2, o)
    for k, o in enumerate(OFFSETS):
        arrive(chunk(gi, o, other), ys.at[k], yr.at[k], y_dev)
    for r in range(4):
        send(block(gi, r, other, core), block(gi, r, other, core), cs.at[4 + r], cr.at[4 + r], c_dev)
    spread_wait(ksa, 0)
    for r in range(4):
        arrive(block(gi, r, half, sib), cs.at[r], cr.at[r], c_dev)
    for r in range(4):
        arrive(block(gi, r, other, sib), cs.at[4 + r], cr.at[4 + r], c_dev)

    def key_block(tt):
        rows = gi[tt].reshape(128, 768)
        tail = rows[:, 640:768].astype(F32)
        dp = (tail[:, 0:1] + tail[:, 1:2]) * SIGMA
        part = jnp.dot(rows[:, 0:640], kw_ref[...], preferred_element_type=F32)
        return (part + dp * ksa[tt].astype(F32)).astype(BF)

    def key_step(k, carry):
        tgt = lax.rem(t + k, 8)
        tt = tau(tgt)
        bsend[k] = key_block(tt)
        copy(bsend.at[k], rsb.at[me_tau], ts.at[8 + k], tr.at[8 + k], (m, tgt)).start()
        return carry

    lax.fori_loop(1, 8, key_step, 0)
    rsb[me_tau] = key_block(me_tau)

    near_wait(gr, zs2, zr2, -4)
    near_wait(gr, zs2, zr2, 4)
    near_wait(gr, zs2, zr2, 8)
    for r in range(4):
        send(block(gr, r, half, core), block(gr, r, half, core), ys2.at[r], yr2.at[r], y_dev)
        send(block(gr, r, half, core), block(gr, r, half, core), cs2.at[r], cr2.at[r], c_dev)

    spread_wait(rsb, 8)
    pre = rsb[0].astype(F32)
    for k in range(1, 8):
        pre = pre + rsb[k].astype(F32)
    act = jnp.maximum(pre, 0.0)
    act = (act * act).astype(BF)
    vd = jnp.sum(act.astype(F32) * vp_ref[...].astype(F32), axis=1, keepdims=True)
    vhigh = vd.astype(BF).astype(F32)
    lanes = lax.broadcasted_iota(jnp.int32, (128, 64), 1)
    tail = jnp.where(lanes == 0, vhigh, jnp.where(lanes == 1, vd - vhigh, 0.0)).astype(BF)
    hid[me_tau] = jnp.concatenate([act, tail], axis=1)
    spread(hid, 16)
    spread(vpa, 24)

    for r in range(4):
        arrive(block(gr, r, other, core), ys2.at[r], yr2.at[r], y_dev)
        send(block(gr, r, other, core), block(gr, r, other, core), cs2.at[4 + r], cr2.at[4 + r], c_dev)
    for r in range(4):
        arrive(block(gr, r, half, sib), cs2.at[r], cr2.at[r], c_dev)
    for r in range(4):
        arrive(block(gr, r, other, sib), cs2.at[4 + r], cr2.at[4 + r], c_dev)

    def weigh(b, carry):
        fcol = gi[b].reshape(128, 768)[:, 640:768].astype(F32)[:, 2:3] * (1.0 / 32.0)
        wgt_k[b] = (fcol * ksa[b].astype(F32)).astype(BF)
        wgt_v[b] = (fcol * gr[b].reshape(128, 1280)[:, 640:1280].astype(F32)).astype(BF)
        return carry

    lax.fori_loop(0, 8, weigh, 0)

    def outer(left, right):
        return lax.dot_general(left, right, (((0,), (0,)), ((), ())), preferred_element_type=F32).astype(BF)

    for j in range(5):
        left = gr[:, :, :, :, :, j * 128 : (j + 1) * 128].reshape(1024, 128)
        ku_ref[j * 128 : (j + 1) * 128, :] = outer(left, wgt_k[...].reshape(1024, 320))

    spread_wait(hid, 16)

    def value_step(b, carry):
        rows = hid[b]
        vd = (rows[:, 320:321].astype(F32) + rows[:, 321:322].astype(F32)) * SIGMA
        part = jnp.dot(rows[:, 0:320], vw_ref[...], preferred_element_type=F32)
        part = part + vd * gr[b].reshape(128, 1280)[:, 640:1280].astype(F32)
        pbuf[b] = part.reshape(2, 2, 2, 16, 640)
        psend[b] = pbuf[b, :, :, sib].astype(BF)
        copy(psend.at[b], rsib.at[b], s_core.at[b], r_core.at[b], c_dev).start()
        return carry

    lax.fori_loop(0, 8, value_step, 0)

    def y_step(b, carry):
        arrive(rsib.at[b], s_core.at[b], r_core.at[b], c_dev)
        ysend[b] = (pbuf[b, :, other, core] + rsib[b, :, other].astype(F32)).astype(BF)
        copy(ysend.at[b], ry.at[b], s_y.at[b], r_y.at[b], y_dev).start()
        return carry

    lax.fori_loop(0, 8, y_step, 0)

    def z_step(b, carry):
        arrive(ry.at[b], s_y.at[b], r_y.at[b], y_dev)
        total = pbuf[b, :, half, core] + rsib[b, :, half].astype(F32) + ry[b].astype(F32)
        zf[b] = total
        zb[b] = total.astype(BF)
        return carry

    lax.fori_loop(0, 8, z_step, 0)

    for k, d in enumerate((1, -1)):
        a, b = klass(d + 4)
        send(zb.at[a, b], rn.at[k], s_z.at[k], r_z.at[k], at_z(d))
    for k, d in enumerate((2, -2)):
        for j, w in enumerate((d, 3 * d)):
            a, b = slot(w)
            i = 2 + 2 * k + j
            send(zb.at[a, b], rn2.at[k, j], s_z.at[i], r_z.at[i], at_z(d))

    spread_wait(vpa, 24)
    right = wgt_v[...].reshape(1024, 640)
    for a, b in ((0, 128), (128, 256), (256, 320)):
        vu_ref[a:b, :] = outer(vpa[:, :, a:b].reshape(1024, b - a), right)

    for k, d in enumerate((1, -1)):
        arrive(rn.at[k], s_z.at[k], r_z.at[k], at_z(-d))
    for k, d in enumerate((2, -2)):
        for j in range(2):
            i = 2 + 2 * k + j
            arrive(rn2.at[k, j], s_z.at[i], r_z.at[i], at_z(-d))

    def gathered(dz):
        a, b = slot(dz)
        za = lax.rem(a, 4)
        return zf[a, b] + rn[0, za].astype(F32) + rn[1, za].astype(F32)

    for k, d in enumerate(FAR):
        total = gathered(d)
        if k < 2:
            total = total + rn2[k, 1].astype(F32)
        fb[k] = total.astype(BF)
        send(fb.at[k], rf.at[k], s_f.at[k], r_f.at[k], at_z(d))
    total = gathered(0) + rn2[0, 0].astype(F32) + rn2[1, 0].astype(F32)
    for k, d in enumerate(FAR):
        arrive(rf.at[k], s_f.at[k], r_f.at[k], at_z(-d))
        total = total + rf[k].astype(F32)
    out_ref[...] = total.astype(BF)

    for c in pending:
        c.wait_send()
    for k in range(1, 8):
        copy(bsend.at[k], rsb.at[me_tau], ts.at[8 + k], tr.at[8 + k], (m, lax.rem(t + k, 8))).wait_send()
    for b in range(8):
        copy(psend.at[b], rsib.at[b], s_core.at[b], r_core.at[b], c_dev).wait_send()
        copy(ysend.at[b], ry.at[b], s_y.at[b], r_y.at[b], y_dev).wait_send()


def body(*args):
    *rest, fitness = args
    vm = pl.BlockSpec(memory_space=pltpu.VMEM)
    dma = pltpu.SemaphoreType.DMA
    return pl.pallas_call(
        kernel,
        out_shape=(
            jax.ShapeDtypeStruct((16, 640), BF),
            jax.ShapeDtypeStruct((640, 320), BF),
            jax.ShapeDtypeStruct((320, 640), BF),
        ),
        in_specs=[vm] * 8,
        out_specs=(vm, vm, vm),
        scratch_shapes=[
            pltpu.VMEM((8, 2, 2, 2, 16, 768), BF),
            pltpu.VMEM((8, 2, 2, 2, 16, 1280), BF),
            pltpu.VMEM((8, 128, 320), BF),
            pltpu.VMEM((8, 128, 320), BF),
            pltpu.VMEM((8, 128, 320), BF),
            pltpu.VMEM((8, 128, 320), BF),
            pltpu.VMEM((8, 128, 384), BF),
            pltpu.VMEM((8, 128, 320), BF),
            pltpu.VMEM((8, 128, 640), BF),
            pltpu.VMEM((8, 2, 2, 2, 16, 640), F32),
            pltpu.VMEM((8, 2, 2, 16, 640), BF),
            pltpu.VMEM((8, 2, 2, 16, 640), BF),
            pltpu.VMEM((8, 2, 16, 640), BF),
            pltpu.VMEM((8, 2, 16, 640), BF),
            pltpu.VMEM((8, 2, 16, 640), F32),
            pltpu.VMEM((8, 2, 16, 640), BF),
            pltpu.VMEM((2, 4, 16, 640), BF),
            pltpu.VMEM((2, 2, 16, 640), BF),
            pltpu.VMEM((3, 16, 640), BF),
            pltpu.VMEM((3, 16, 640), BF),
        ]
        + [dma((n,)) for n in (15, 15, 16, 16, 8, 8, 15, 15, 4, 4, 8, 8, 32, 32, 8, 8, 8, 8, 6, 6, 3, 3)],
        compiler_params=pltpu.CompilerParams(
            collective_id=0, has_side_effects=True, vmem_limit_bytes=48 * 2**20
        ),
        cost_estimate=pl.CostEstimate(flops=1_700_000_000, bytes_accessed=4_000_000, transcendentals=0),
        name="step",
    )(*rest, fitness.reshape(1, 16))


def solution(mesh):
    placed = (
        P("member", "tensor"), P("tensor", "member"), P("member", "tensor"), P("member", "tensor"),
        P("tensor", "member"), P("tensor", "member"), P("member", "tensor"), P("member"),
    )
    return jax.shard_map(
        body,
        mesh=mesh,
        in_specs=placed,
        out_specs=(P("member", "tensor"), P("tensor", "member"), P("member", "tensor")),
        check_vma=False,
    )
```

time: 708 us -> 117 us (0.17)
  blocking collectives: 354 us -> 0 us
  waiting for transfers between devices: 321 us -> 0 us
  Pallas kernels: 0 us -> 112 us
  between operations: 15.8 us -> 0.75 us
  matrix products: 9.93 us -> 0 us
    all_gather x3 -> x0, waiting for transfers between devices: 281 us -> none  [the longest x1 148 us: body(): lax.all_gather(inputs, 'member', axis=0, tiled=True)]
    unnamed x3 -> x0, blocking collectives: 274 us -> none
    pallas_call x0 -> x1, Pallas kernels: none -> 112 us  [body(): pl.pallas_call(kernel, out_shape=(jax.ShapeDtypeStruct((16, 640), BF), ja...]
    all_gather x3 -> x0, blocking collectives: 79.6 us -> none  [the longest x1 27 us: body(): lax.all_gather(hidden, 'tensor', axis=0, tiled=True)]
    reduce_scatter x2 -> x0, waiting for transfers between devices: 37.9 us -> none  [the longest x1 25.3 us: body(): lax.psum_scatter(key_partial, 'tensor', scatter_dimension=0, tiled=True)]
    dot_general x4 -> x0, matrix products: 9.93 us -> none  [the longest x2 4.28 us: outer_sum(): lax.dot_general(probe_rows, weighted, (((0,), (0,)), ((), ())), preferred...]
  transfers between devices with their start and end apart: 5 -> 0, of which waited for: 4 -> 0; matrix products, arithmetic and copies ran while one was open for 2% -> 0% of each run, Pallas kernels for 0% -> 0%
where the time goes in v1:
time: 117 us
  Pallas kernels  112 us (96%)
  local copies, waits for them, and re-layouts  4.8 us (4%)
    pallas_call x1, Pallas kernels, body(): pl.pallas_call(kernel, out_shape=(jax.ShapeDtypeStruct((16, 640), BF), ja...  112 us
    unnamed x17, local copies, waits for them, and re-layouts  3.85 us

profile of v1, /device:TPU:4, one launch (start us, length us, event | category | flops | bytes accessed | tf_op | source)
XLA Modules:
  0.0 117.2 jit_solution(8611031922797361372)
XLA Ops:
  0.6 0.0 copy-start.5
  0.6 1.0 copy.12.ks_ref
  1.7 0.0 copy-done.5
  1.7 0.1 copy.13.vp_ref
  1.8 0.0 copy-start
  1.8 0.0 copy-start.1
  1.8 0.0 copy-start.2
  1.9 0.0 copy-start.3
  1.9 0.0 copy-start.4
  1.9 1.3 %copy.11.kw_ref = bf16[640,320]{1,0:T(8,128)(2,1)S(1)} copy(bf16[640,320]{0,1:T(8,128)(2,1)} %param.9) | data formatting | bytes 819200 | tf_op args[1]
  3.2 0.0 copy-done
  3.2 0.0 copy-done.1
  3.2 0.0 copy-done.2
  3.2 0.0 copy-done.3
  3.2 0.0 copy-done.4
  3.2 111.7 %step.1 = (bf16[16,640]{1,0:T(8,128)(2,1)S(1)}, bf16[640,320]{1,0:T(8,128)(2,1)S(1)}, bf16[320,640]{1,0:T(8,128)(2,1)S(1)}) custom-call(bf16[16,640]{1,0:T(8,128)(2,1)S(1)} %copy-done.1, bf16[640,320]{1,0:T(8,128)(2,1)S(1)} %copy.11.kw_ref, bf16[320,640]{1,0:T(8,128)(2,1)S(1)} %copy-done, bf16[16,640]{1,0:T(8,128)(2,1)S(1)} %copy-done.2, ...), custom_call_target="tpu_custom_call" | custom-call | flops 1700000000 | bytes 4000000 | tf_op jit(solution)/shard_map/step/pallas_call | solution.py:310
  114.9 1.0 copy.14
  115.9 0.6 copy.17
  116.5 0.8 copy.18
Async XLA Ops:
  0.6 1.0 copy-start.5
  1.8 1.4 %copy-start = (bf16[320,640]{1,0:T(8,128)(2,1)S(1)}, bf16[320,640]{1,0:T(8,128)(2,1)}, u32[]{:S(2)}) copy-start(bf16[320,640]{1,0:T(8,128)(2,1)} %vw_ref.1) | copy-start | bytes 1228804
  1.8 1.4 %copy-start.1 = (bf16[16,640]{1,0:T(8,128)(2,1)S(1)}, bf16[16,640]{1,0:T(8,128)(2,1)}, u32[]{:S(2)}) copy-start(bf16[16,640]{1,0:T(8,128)(2,1)} %x_ref.1) | copy-start | bytes 61444
  1.8 1.4 %copy-start.2 = (bf16[16,640]{1,0:T(8,128)(2,1)S(1)}, bf16[16,640]{1,0:T(8,128)(2,1)}, u32[]{:S(2)}) copy-start(bf16[16,640]{1,0:T(8,128)(2,1)} %kp_ref.1) | copy-start | bytes 61444
  1.9 1.4 %copy-start.3 = (bf16[16,640]{1,0:T(8,128)(2,1)S(1)}, bf16[16,640]{1,0:T(8,128)(2,1)}, u32[]{:S(2)}) copy-start(bf16[16,640]{1,0:T(8,128)(2,1)} %vs_ref.1) | copy-start | bytes 61444
  1.9 1.4 %copy-start.4 = (bf16[16]{0:T(256)(128)(2,1)S(1)}, bf16[16]{0:T(256)(128)(2,1)}, u32[]{:S(2)}) copy-start(bf16[16]{0:T(256)(128)(2,1)} %param.15) | copy-start | bytes 100

commit v2 on v1

v2 whole, which is shorter than its diff:
```python
import functools

import jax
import jax.numpy as jnp
from jax import lax
from jax.experimental import pallas as pl
from jax.experimental.pallas import tpu as pltpu
from jax.sharding import PartitionSpec as P

BF, F32 = jnp.bfloat16, jnp.float32
MESH = pl.DeviceIdType.MESH
SIGMA = 0.005

FAR = (4, -4, 8)
NEAR = (
    (1, 0), (-1, 0), (2, 0), (-2, 0),
    (1, -4), (-1, -4), (2, -4),
    (1, 4), (-1, 4), (-2, 4),
    (1, 8), (-1, 8),
)
OFFSETS = (0, -1, 1, -2, 2, -4, 4, -5, 3, -3, 5, -6, 6, 8, 7, -7)


def kernel(
    x_ref, kw_ref, vw_ref, kp_ref, ks_ref, vp_ref, vs_ref, f_ref,
    out_ref, ku_ref, vu_ref,
    kw, vw, fv, vsv, gi, gr, ksa, vpa, bsend, rsb, hid, wgt_k, pbuf, psend, rsib, ysend, ry, zf, zb, rn, rn2, fb, rf, vdt, vds, vdr, mt, mts, mtr,
    ls, zs, zr, ys, yr, cs, cr, gs, gv, ys2, yr2, cs2, cr2, ts, tr, s_core, r_core, s_y, r_y, s_z, r_z, s_f, r_f, s_vd, r_vd, s_mt, r_mt,
):
    m, t = lax.axis_index("member"), lax.axis_index("tensor")
    z, half, core = m // 4, (m // 2) % 2, m % 2
    other, sib = 1 - half, 1 - core

    def at_z(dz):
        return (lax.rem(z + dz + 16, 16) * 4 + half * 2 + core, t)

    y_dev = (z * 4 + other * 2 + core, t)
    c_dev = (z * 4 + half * 2 + sib, t)

    def tau(tt):
        return lax.rem(tt, 2) * 4 + tt // 2

    def slot(dz):
        zz = lax.rem(z + dz + 16, 16)
        return (lax.rem(zz, 4) // 2) * 4 + zz // 4, lax.rem(zz, 2)

    def klass(r):
        cc = lax.rem(z + r, 4)
        return pl.ds((cc // 2) * 4, 4), lax.rem(cc, 2)

    def cols(tt):
        return pl.ds(pl.multiple_of(tt * 128, 128), 128)

    parts = (pl.ds(0, 160), pl.ds(160, 176))

    def at_block(buf, tt, part=None):
        if buf is vpa:
            return buf.at[:, cols(tt)]
        return buf.at[tt] if part is None else buf.at[tt, parts[part]]

    me_tau = tau(t)
    pending = []

    def copy(src, dst, ssem, rsem, dev):
        return pltpu.make_async_remote_copy(
            src_ref=src, dst_ref=dst, send_sem=ssem, recv_sem=rsem, device_id=dev, device_id_type=MESH
        )

    def send(src, dst, ssem, rsem, dev):
        c = copy(src, dst, ssem, rsem, dev)
        c.start()
        pending.append(c)

    def arrive(dst, ssem, rsem, dev):
        copy(dst, dst, ssem, rsem, dev).wait_recv()

    bar = pltpu.get_barrier_semaphore()
    partners = [at_z(d) for d in (8, 4, -4, 1, -1, 2, -2)] + [y_dev, c_dev]
    partners += [(m, lax.rem(t + k, 8)) for k in range(1, 8)]
    for dev in partners:
        pl.semaphore_signal(bar, inc=1, device_id=dev, device_id_type=MESH)

    def chunk(g, dz, hh=None, cc=None):
        a, b = slot(dz)
        return g.at[a, b, half if hh is None else hh, core if cc is None else cc]

    def block(g, r, hh, cc):
        a, b = klass(r)
        return g.at[a, b, hh, cc]

    st, sl = slot(0)
    mine_i, mine_r = gi.at[st, sl, half, core], gr.at[st, sl, half, core]
    loads = [
        pltpu.make_async_copy(src, dst, ls.at[k])
        for k, (src, dst) in enumerate(
            (
                (x_ref, mine_i), (kp_ref, mine_r.at[:, 0:640]), (vs_ref, vsv),
                (ks_ref, ksa.at[me_tau]), (vp_ref, vpa.at[:, cols(me_tau)]), (f_ref, fv), (kw_ref, kw), (vw_ref, vw),
            )
        )
    ]
    for c in loads:
        c.start()

    first = sl * 64 + half * 32 + core * 16
    spot = lax.broadcasted_iota(jnp.int32, (16, 128), 1) == first + lax.broadcasted_iota(jnp.int32, (16, 128), 0)

    def place(col):
        return jnp.sum(jnp.where(spot, col, 0.0), axis=0, keepdims=True)

    mt[...] = jnp.zeros((16, 128), F32)
    for c in loads[0:6]:
        c.wait()
    fit = jnp.broadcast_to(fv[...].astype(F32), (16, 16))
    row, lane = (lax.broadcasted_iota(jnp.int32, (16, 16), d) for d in (0, 1))
    fit = jnp.sum(jnp.where(row == lane, fit, 0.0), axis=1, keepdims=True) * (1.0 / 32.0)
    dots = jnp.sum(mine_i[...].astype(F32) * mine_r[:, 0:640].astype(F32), axis=1, keepdims=True)
    mt[pl.ds(st, 1)] = place(dots * SIGMA)
    mt[pl.ds(8 + st, 1)] = place(fit)
    mine_r[:, 640:1280] = (fit * vsv[...].astype(F32)).astype(BF)

    pl.semaphore_wait(bar, len(partners))

    def near_send(o):
        for k, (d, oo) in enumerate(NEAR):
            if oo == o:
                send(chunk(gi, o), chunk(gi, o), zs.at[3 + k], zr.at[3 + k], at_z(d))

    def far_wait(k):
        arrive(chunk(gi, -FAR[k]), zs.at[k], zr.at[k], at_z(-FAR[k]))

    def near_wait(o):
        for k, (d, oo) in enumerate(NEAR):
            if oo == o:
                arrive(chunk(gi, oo - d), zs.at[3 + k], zr.at[3 + k], at_z(-d))
                y_send(oo - d)

    def y_send(dz):
        dz = dz if dz <= 8 else dz - 16
        k = OFFSETS.index(dz)
        send(chunk(gi, dz), chunk(gi, dz), ys.at[k], yr.at[k], y_dev)

    ty = lax.rem(t + 4, 8)

    def along_x(k):
        return (t // 4) * 4 + lax.rem(t + k, 4)

    def source(k):
        return lax.rem((t // 4) * 4 + lax.rem(t + 4 - lax.rem(k, 4), 4) + 4 * (k // 4), 8)

    def spread(buf, base, part=None):
        b = at_block(buf, me_tau, part)
        send(b, b, ts.at[base + 4], tr.at[base + 4], (m, ty))
        for k in (2, 1, 3):
            send(b, b, ts.at[base + k], tr.at[base + k], (m, along_x(k)))

    def pass_on(buf, base, part=None, to=(2, 1, 3)):
        b = at_block(buf, tau(ty), part)
        arrive(b, ts.at[base + 4], tr.at[base + 4], (m, ty))
        for k in to:
            send(b, b, ts.at[base + 4 + k], tr.at[base + 4 + k], (m, along_x(k)))

    def pass_back(buf, base, part):
        spread_wait(buf, base, 2, part)
        b = at_block(buf, tau(along_x(2)), part)
        send(b, b, ts.at[base + 6], tr.at[base + 6], (m, ty))

    def spread_wait(buf, base, k, part=None):
        frm = source(k)
        arrive(at_block(buf, tau(frm), part), ts.at[base + k], tr.at[base + k], (m, frm))

    def ring_send(s):
        for hh in (0, 1):
            for sign in (1, -1):
                if s == 8 and (hh == 0) != (sign > 0):
                    continue
                i = (sign < 0) * 16 + (s - 1) * 2 + hh
                c = chunk(gr, -sign * (s - 1), hh)
                send(c, c, gs.at[i], gv.at[i], at_z(sign))

    def ring_wait(s):
        for hh in (0, 1):
            for sign in (1, -1):
                if s == 8 and (hh == 0) != (sign > 0):
                    continue
                i = (sign < 0) * 16 + (s - 1) * 2 + hh
                c = chunk(gr, -sign * s, hh)
                arrive(c, gs.at[i], gv.at[i], at_z(-sign))
                if s < 7 or (s == 7 and (hh == 0) == (sign > 0)):
                    n = i + 2
                    send(c, c, gs.at[n], gv.at[n], at_z(sign))
                send(c, c, cs2.at[i], cr2.at[i], c_dev)

    def ring_end():
        for s in range(1, 9):
            for hh in (0, 1):
                for sign in (1, -1):
                    if s == 8 and (hh == 0) != (sign > 0):
                        continue
                    i = (sign < 0) * 16 + (s - 1) * 2 + hh
                    arrive(chunk(gr, -sign * s, hh, sib), cs2.at[i], cr2.at[i], c_dev)
        for hh in (0, 1):
            arrive(chunk(gr, 0, hh, sib), cs2.at[32 + hh], cr2.at[32 + hh], c_dev)

    def round_of(tile, held, got, ssem, rsem):
        def begin(n, *links):
            held[n] = tile[...]
            for k, dev in links:
                send(held.at[n], got.at[k], ssem.at[k], rsem.at[k], dev)

        def end(*ks):
            for k in ks:
                arrive(got.at[k], ssem.at[k], rsem.at[k], c_dev)
                tile[...] += got[k]

        return begin, end

    mt_send, mt_add = round_of(mt, mts, mtr, s_mt, r_mt)
    vd_send, vd_add = round_of(vdt, vds, vdr, s_vd, r_vd)
    near_links = ((2, at_z(1)), (3, at_z(-1)), (4, at_z(-2)))
    far_links = ((5, at_z(4)), (6, at_z(-4)), (7, at_z(8)))

    mt_send(0, *far_links)
    for k in (2, 0, 1):
        send(chunk(gi, 0), chunk(gi, 0), zs.at[k], zr.at[k], at_z(FAR[k]))
    near_send(0)
    y_send(0)
    send(mine_r, mine_r, ys2, yr2, y_dev)
    spread(ksa, 0)

    for k, o in ((0, -4), (1, 4)):
        far_wait(k)
        near_send(o)
    near_wait(0)
    for o in (-4, 4):
        y_send(o)
    far_wait(2)
    near_send(8)
    y_send(8)
    mt_add(5, 6, 7)
    mt_send(1, *near_links)
    theirs = chunk(gr, 0, other)
    arrive(theirs, ys2, yr2, y_dev)
    ring_send(1)
    for hh in (0, 1):
        c = chunk(gr, 0, hh)
        send(c, c, cs2.at[32 + hh], cr2.at[32 + hh], c_dev)
    pass_on(ksa, 0)
    near_wait(-4)
    near_wait(4)
    near_wait(8)
    mt_add(2, 3, 4)
    mt_send(2, (1, y_dev))
    for r in range(4):
        send(block(gi, r, half, core), block(gi, r, half, core), cs.at[r], cr.at[r], c_dev)
    ring_wait(1)
    for r in range(4):
        for o in OFFSETS:
            if (o - r) % 4 == 0:
                k = OFFSETS.index(o)
                arrive(chunk(gi, o, other), ys.at[k], yr.at[k], y_dev)
        send(block(gi, r, other, core), block(gi, r, other, core), cs.at[4 + r], cr.at[4 + r], c_dev)
    mt_add(1)
    mt_send(3, (0, c_dev))
    for k in (1, 3, 2):
        spread_wait(ksa, 0, k)
        spread_wait(ksa, 0, k + 4)
    for c in loads[6:]:
        c.wait()
    for r in range(4):
        arrive(block(gi, r, half, sib), cs.at[r], cr.at[r], c_dev)
    for r in range(4):
        arrive(block(gi, r, other, sib), cs.at[4 + r], cr.at[4 + r], c_dev)

    mt_add(0)
    ring_wait(2)
    def key_block(tt):
        rows = gi[tt].reshape(128, 640)
        dp = mt[pl.ds(tt, 1)]
        part = lax.dot_general(
            kw[...], rows, (((1,), (1,)), ((), ())), preferred_element_type=F32
        )
        return (part + dp * ksa[tt].astype(F32)).astype(BF)

    def key_copy(k, h):
        tgt = lax.rem(t + k, 8)
        u = pl.ds(h * 160, 160)
        return copy(bsend.at[k, u], rsb.at[me_tau, u], ts.at[32 + 8 * h + k], tr.at[32 + 8 * h + k], (m, tgt))

    def key_step(i, carry):
        k = 7 - i
        bsend[k] = key_block(tau(lax.rem(t + k, 8)))
        key_copy(k, 0).start()
        return carry

    lax.fori_loop(0, 7, key_step, 0)
    for k in range(7, 0, -1):
        key_copy(k, 1).start()
    rsb[me_tau] = key_block(me_tau)

    def weigh_k(b, carry):
        wgt_k[:, cols(b)] = (mt[pl.ds(8 + b, 1)] * ksa[b].astype(F32)).astype(BF)
        return carry

    lax.fori_loop(0, 8, weigh_k, 0)
    ring_wait(3)
    def value_step(p, k):
        b = tau(source(k))
        tail = hid[b, 320:336].astype(F32)
        vdt[pl.ds(b, 1)] = tail[0:1] + tail[1:2]
        part = lax.dot_general(
            hid[b, 0:320], vw[...], (((0,), (0,)), ((), ())), preferred_element_type=F32
        )
        pbuf[p] = part.reshape(2, 2, 2, 16, 640)
        psend[p] = pbuf[p, :, :, sib].astype(BF)
        copy(psend.at[p], rsib.at[p], s_core.at[p], r_core.at[p], c_dev).start()

    def y_step(p):
        arrive(rsib.at[p], s_core.at[p], r_core.at[p], c_dev)
        ysend[p] = (pbuf[p, :, other, core] + rsib[p, :, other].astype(F32)).astype(BF)
        copy(ysend.at[p], ry.at[p], s_y.at[p], r_y.at[p], y_dev).start()

    def z_step(p, k):
        b = tau(source(k))
        arrive(ry.at[p], s_y.at[p], r_y.at[p], y_dev)
        total = pbuf[p, :, half, core] + rsib[p, :, half].astype(F32) + ry[p].astype(F32)
        zf[b] = total
        zb[b] = total.astype(BF)

    vd = jnp.zeros((1, 128), F32)
    for h in (0, 1):
        u = pl.ds(h * 160, 160)
        for k in range(1, 8):
            frm = lax.rem(t + 8 - k, 8)
            i = 32 + 8 * h + k
            arrive(rsb.at[tau(frm), u], ts.at[i], tr.at[i], (m, frm))
        pre = rsb[0, u].astype(F32)
        for k in range(1, 8):
            pre = pre + rsb[k, u].astype(F32)
        act = jnp.maximum(pre, 0.0)
        act = (act * act).astype(BF)
        hid[me_tau, u] = act
        vd = vd + jnp.sum(act.astype(F32) * vpa[u, cols(me_tau)].astype(F32), axis=0, keepdims=True)
        if h == 1:
            vhigh = vd.astype(BF).astype(F32)
            line = lax.broadcasted_iota(jnp.int32, (16, 128), 0)
            tail = jnp.where(line == 0, vhigh, jnp.where(line == 1, vd - vhigh, 0.0))
            hid[me_tau, 320:336] = tail.astype(BF)
        spread(hid, 8 + 8 * h, h)
        if h == 0:
            ring_wait(4)
    pass_on(hid, 8, 0, (1, 3))
    value_step(0, 0)
    ring_wait(5)
    pass_on(hid, 16, 1, (1, 3))
    pass_back(hid, 8, 0)
    value_step(1, 4)
    y_step(0)
    pass_back(hid, 16, 1)
    value_step(2, 2)
    y_step(1)

    def value_loop(p, carry):
        k = 2 * p - 5
        spread_wait(hid, 8, k, 0)
        spread_wait(hid, 16, k, 1)
        value_step(p, k)
        y_step(p - 1)
        return carry

    lax.fori_loop(3, 5, value_loop, 0)
    ring_wait(6)
    lax.fori_loop(5, 7, value_loop, 0)
    spread_wait(hid, 8, 6, 0)
    spread_wait(hid, 16, 6, 1)
    value_step(7, 6)
    y_step(6)
    vd_send(0, (0, c_dev))
    y_step(7)
    vd_add(0)
    vd_send(1, (1, y_dev))
    spread(vpa, 24)
    ring_wait(7)
    z_step(0, 0)
    z_step(1, 4)
    z_step(2, 2)

    def z_loop(p, carry):
        z_step(p, 2 * p - 5)
        return carry

    lax.fori_loop(3, 5, z_loop, 0)
    ring_wait(8)
    lax.fori_loop(5, 7, z_loop, 0)
    z_step(7, 6)

    spans = (pl.ds(0, 384), pl.ds(384, 256))

    def near_copies(c):
        w = spans[c]
        out = []
        for k, d in enumerate((1, -1)):
            a, b = klass(d + 4)
            out.append((zb.at[a, b, :, w], rn.at[k, :, :, w], d))
        for k, d in enumerate((2, -2)):
            for j, v in enumerate((d, 3 * d)):
                a, b = slot(v)
                out.append((zb.at[a, b, :, w], rn2.at[k, j, :, w], d))
        return out

    for c in (0, 1):
        for i, (src, dst, d) in enumerate(near_copies(c)):
            send(src, dst, s_z.at[6 * c + i], r_z.at[6 * c + i], at_z(d))
    vd_add(1)
    vd_send(2, *near_links)
    pass_on(vpa, 24)

    def gathered(dz, w):
        a, b = slot(dz)
        za = lax.rem(a, 4)
        return zf[a, b, :, w] + rn[0, za, :, w].astype(F32) + rn[1, za, :, w].astype(F32)

    def far_copy(k, c):
        w = spans[c]
        return fb.at[k, :, w], rf.at[k, :, w], s_f.at[3 * c + k], r_f.at[3 * c + k], at_z(FAR[k])

    for c in (0, 1):
        w = spans[c]
        for i, (_, dst, d) in enumerate(near_copies(c)):
            arrive(dst, s_z.at[6 * c + i], r_z.at[6 * c + i], at_z(-d))
        for k in (2, 0, 1):
            total = gathered(FAR[k], w)
            if k < 2:
                total = total + rn2[k, 1, :, w].astype(F32)
            fb[k, :, w] = total.astype(BF)
            send(*far_copy(k, c))
    vd_add(2, 3, 4)
    vd_send(3, *far_links)
    ring_end()

    def outer(left, right):
        return jnp.dot(left, right, preferred_element_type=F32).astype(BF)

    for a in range(0, 320, 64):
        ku_ref[a : a + 64] = outer(wgt_k[a : a + 64], gr[:, :, :, :, :, 0:640].reshape(1024, 640))
    for k in (1, 3, 2):
        spread_wait(vpa, 24, k)
        spread_wait(vpa, 24, k + 4)
    right = gr[:, :, :, :, :, 640:1280].reshape(1024, 640)
    for a in range(0, 320, 64):
        vu_ref[a : a + 64] = outer(vpa[a : a + 64], right)

    for c in pending:
        c.wait_send()
    for k in range(1, 8):
        for h in (0, 1):
            key_copy(k, h).wait_send()
    for b in range(8):
        copy(psend.at[b], rsib.at[b], s_core.at[b], r_core.at[b], c_dev).wait_send()
        copy(ysend.at[b], ry.at[b], s_y.at[b], r_y.at[b], y_dev).wait_send()
    vd_add(5, 6, 7)
    vd = SIGMA * jnp.sum(jnp.where(spot, vdt[pl.ds(st, 1)], 0.0), axis=1, keepdims=True)
    for c, w in enumerate(spans):
        total = gathered(0, w) + rn2[0, 0, :, w].astype(F32) + rn2[1, 0, :, w].astype(F32)
        total = total + vd * vsv[:, w].astype(F32)
        for k in (0, 1, 2):
            _, dst, ssem, rsem, dev = far_copy(k, c)
            arrive(dst, ssem, rsem, dev)
            total = total + rf[k, :, w].astype(F32)
        out_ref[:, w] = total.astype(BF)


def store(*refs):
    copies = [pltpu.make_async_copy(a, b, refs[6].at[k]) for k, (a, b) in enumerate(zip(refs[0:3], refs[3:6]))]
    for c in copies:
        c.start()
    for c in copies:
        c.wait()


def body(*args):
    x, kw, vw, kp, ks, vp, vs, fitness = args
    vm = pl.BlockSpec(memory_space=pltpu.VMEM)
    dma = pltpu.SemaphoreType.DMA
    args = (pltpu.with_memory_space_constraint(a, pltpu.HBM) for a in (x, kw.T, vw, kp, ks.T, vp.T, vs, fitness.reshape(1, 16)))
    out, ku, vu = pl.pallas_call(
        kernel,
        out_shape=(
            jax.ShapeDtypeStruct((16, 640), BF),
            jax.ShapeDtypeStruct((320, 640), BF),
            jax.ShapeDtypeStruct((320, 640), BF),
        ),
        in_specs=[pl.BlockSpec(memory_space=pltpu.HBM)] * 8,
        out_specs=(vm, vm, vm),
        scratch_shapes=[
            pltpu.VMEM((320, 640), BF),
            pltpu.VMEM((320, 640), BF),
            pltpu.VMEM((1, 16), BF),
            pltpu.VMEM((16, 640), BF),
            pltpu.VMEM((8, 2, 2, 2, 16, 640), BF),
            pltpu.VMEM((8, 2, 2, 2, 16, 1280), BF),
            pltpu.VMEM((8, 320, 128), BF),
            pltpu.VMEM((320, 1024), BF),
            pltpu.VMEM((8, 320, 128), BF),
            pltpu.VMEM((8, 320, 128), BF),
            pltpu.VMEM((8, 336, 128), BF),
            pltpu.VMEM((320, 1024), BF),
            pltpu.VMEM((8, 2, 2, 2, 16, 640), F32),
            pltpu.VMEM((8, 2, 2, 16, 640), BF),
            pltpu.VMEM((8, 2, 2, 16, 640), BF),
            pltpu.VMEM((8, 2, 16, 640), BF),
            pltpu.VMEM((8, 2, 16, 640), BF),
            pltpu.VMEM((8, 2, 16, 640), F32),
            pltpu.VMEM((8, 2, 16, 640), BF),
            pltpu.VMEM((2, 4, 16, 640), BF),
            pltpu.VMEM((2, 2, 16, 640), BF),
            pltpu.VMEM((3, 16, 640), BF),
            pltpu.VMEM((3, 16, 640), BF),
            pltpu.VMEM((8, 128), F32),
            pltpu.VMEM((4, 8, 128), F32),
            pltpu.VMEM((8, 8, 128), F32),
            pltpu.VMEM((16, 128), F32),
            pltpu.VMEM((4, 16, 128), F32),
            pltpu.VMEM((8, 16, 128), F32),
        ]
        + [dma((n,)) for n in (8, 15, 15, 16, 16, 8, 8, 32, 32)]
        + [dma(()), dma(())]
        + [dma((n,)) for n in (34, 34, 48, 48, 8, 8, 8, 8, 12, 12, 6, 6, 8, 8, 8, 8)],
        compiler_params=pltpu.CompilerParams(
            collective_id=0, has_side_effects=True, vmem_limit_bytes=48 * 2**20
        ),
        cost_estimate=pl.CostEstimate(flops=1_700_000_000, bytes_accessed=4_000_000, transcendentals=0),
        name="step",
    )(*args)
    anywhere = pl.BlockSpec(memory_space=pl.ANY)
    out, ku, vu = pl.pallas_call(
        store,
        out_shape=tuple(jax.ShapeDtypeStruct(a.shape, BF) for a in (out, ku, vu)),
        in_specs=[anywhere] * 3,
        out_specs=(anywhere,) * 3,
        scratch_shapes=[dma((3,))],
        compiler_params=pltpu.CompilerParams(vmem_limit_bytes=2 * 2**20),
        name="store",
    )(out, ku, vu)
    return out, ku.T, vu


def solution(mesh):
    placed = (
        P("member", "tensor"), P("tensor", "member"), P("member", "tensor"), P("member", "tensor"),
        P("tensor", "member"), P("tensor", "member"), P("member", "tensor"), P("member"),
    )
    return jax.shard_map(
        body,
        mesh=mesh,
        in_specs=placed,
        out_specs=(P("member", "tensor"), P("tensor", "member"), P("member", "tensor")),
        check_vma=False,
    )
```

time: 117 us -> 79.1 us (0.68)
  the two profiles are of different devices: /device:TPU:4 before, /device:TPU:64 now
where the time goes in v2:
time: 79.1 us; the launch traced here: 78.9 us
  Pallas kernels  78.3 us (99%)
    pallas_call x1, Pallas kernels, body(): pl.pallas_call(kernel, out_shape=(jax.ShapeDtypeStruct((16, 640), BF), ja...  77.4 us

profile of v2, /device:TPU:64, one launch (start us, length us, event | category | flops | bytes accessed | tf_op | source)
XLA Modules:
  0.0 78.9 jit_solution(11077981239469981852)
XLA Ops:
  0.6 77.4 %step.1 = (bf16[16,640]{1,0:T(8,128)(2,1)S(1)}, bf16[320,640]{1,0:T(8,128)(2,1)S(1)}, bf16[320,640]{1,0:T(8,128)(2,1)S(1)}) custom-call(bf16[16,640]{1,0:T(8,128)(2,1)} %x_ref.1, bf16[320,640]{1,0:T(8,128)(2,1)} %bitcast.5, bf16[320,640]{1,0:T(8,128)(2,1)} %vw_ref.1, bf16[16,640]{1,0:T(8,128)(2,1)} %kp_ref.1, bf16[320,128]{1,0:T(8,128)(2,1)} %bitcast.7, ...), custom_call_target="tpu_custom_call" | custom-call | flops 1700000000 | bytes 4000000 | tf_op jit(solution)/shard_map/step/pallas_call | solution.py:486
  78.0 0.9 %store.1 = (bf16[16,640]{1,0:T(8,128)(2,1)}, bf16[320,640]{1,0:T(8,128)(2,1)}, bf16[320,640]{1,0:T(8,128)(2,1)}) custom-call(bf16[16,640]{1,0:T(8,128)(2,1)S(1)} %get-tuple-element.9.refs_0_, bf16[320,640]{1,0:T(8,128)(2,1)S(1)} %get-tuple-element.10.refs_1_, bf16[320,640]{1,0:T(8,128)(2,1)S(1)} %get-tuple-element.11.refs_2_), custom_call_target="tpu_custom_call" | custom-call | tf_op jit(solution)/shard_map/store/pallas_call | solution.py:536

commit v3 on v2

--- a/solution.py
+++ b/solution.py
@@ -25,7 +25,7 @@
     x_ref, kw_ref, vw_ref, kp_ref, ks_ref, vp_ref, vs_ref, f_ref,
     out_ref, ku_ref, vu_ref,
     kw, vw, fv, vsv, gi, gr, ksa, vpa, bsend, rsb, hid, wgt_k, pbuf, psend, rsib, ysend, ry, zf, zb, rn, rn2, fb, rf, vdt, vds, vdr, mt, mts, mtr,
-    ls, zs, zr, ys, yr, cs, cr, gs, gv, ys2, yr2, cs2, cr2, ts, tr, s_core, r_core, s_y, r_y, s_z, r_z, s_f, r_f, s_vd, r_vd, s_mt, r_mt,
+    ls, ss, rr, gv, tr, r_core, r_y,
 ):
     m, t = lax.axis_index("member"), lax.axis_index("tensor")
     z, half, core = m // 4, (m // 2) % 2, m % 2
@@ -59,7 +59,32 @@
         return buf.at[tt] if part is None else buf.at[tt, parts[part]]
 
     me_tau = tau(t)
-    pending = []
+
+    class Shared:
+        def __init__(self, ref, which):
+            self.ref, self.which, self.at = ref, which, self
+
+        def __getitem__(self, k):
+            return self.ref.at[self.which(k) if callable(self.which) else self.which]
+
+    zs = Shared(ss, lambda k: 0 if k < 7 else 1)
+    ys, cs, cs2, s_ks, s_vp, s_key, s_core, s_y, s_mt, s_vd = (Shared(ss, n) for n in range(2, 12))
+    gs = Shared(ss, lambda k: 12 if k in (14, 31) else 13)
+    s_hid = Shared(ss, lambda k: 14 + k // 8)
+    s_z = Shared(ss, lambda k: 16 + k // 6)
+    s_f = Shared(ss, lambda k: 18 + k // 3)
+    ys2, yr2 = ss.at[20], rr.at[0]
+    zr = Shared(rr, lambda k: 1 + k if k < 3 else 4 if k < 7 else 5 if k < 13 else 6)
+    yr = Shared(rr, lambda k: 7 + OFFSETS[k] % 4)
+    cr, cr2 = Shared(rr, 11), Shared(rr, 12)
+    r_ks = Shared(rr, lambda k: 13 if k == 4 else 14)
+    r_vp = Shared(rr, lambda k: 15 if k == 4 else 16)
+    r_key = Shared(rr, lambda h: 17 + h)
+    r_z = Shared(rr, lambda k: 19 + 2 * (k // 6) + (0 if k % 6 < 2 else 1))
+    r_f = Shared(rr, lambda k: 23 + k // 3)
+    tiles = lambda k: k if k < 2 else 2 if k < 5 else 3
+    r_vd = Shared(rr, lambda k: 25 + tiles(k))
+    r_mt = Shared(tr, lambda k: 16 + tiles(k))
 
     def copy(src, dst, ssem, rsem, dev):
         return pltpu.make_async_remote_copy(
@@ -67,9 +92,10 @@
         )
 
     def send(src, dst, ssem, rsem, dev):
-        c = copy(src, dst, ssem, rsem, dev)
-        c.start()
-        pending.append(c)
+        copy(src, dst, ssem, rsem, dev).start()
+
+    def sent(ref, sem):
+        copy(ref, ref, sem, sem, c_dev).wait_send()
 
     def arrive(dst, ssem, rsem, dev):
         copy(dst, dst, ssem, rsem, dev).wait_recv()
@@ -129,11 +155,12 @@
     def far_wait(k):
         arrive(chunk(gi, -FAR[k]), zs.at[k], zr.at[k], at_z(-FAR[k]))
 
-    def near_wait(o):
-        for k, (d, oo) in enumerate(NEAR):
-            if oo == o:
-                arrive(chunk(gi, oo - d), zs.at[3 + k], zr.at[3 + k], at_z(-d))
-                y_send(oo - d)
+    def near_wait(*os):
+        came = [(k, oo - d) for k, (d, oo) in enumerate(NEAR) if oo in os]
+        k = 3 + came[0][0]
+        arrive(gi.at[pl.ds(0, len(came)), 0, 0, 0], zs.at[k], zr.at[k], c_dev)
+        for _, dz in came:
+            y_send(dz)
 
     def y_send(dz):
         dz = dz if dz <= 8 else dz - 16
@@ -148,26 +175,34 @@
     def source(k):
         return lax.rem((t // 4) * 4 + lax.rem(t + 4 - lax.rem(k, 4), 4) + 4 * (k // 4), 8)
 
+    def spread_sems(buf, base):
+        if buf is ksa:
+            return s_ks, r_ks
+        return (s_vp, r_vp) if buf is vpa else (Shared(ss, 14 + base // 8), tr)
+
+    def spread_copy(buf, base, part, k, frm, to):
+        b = at_block(buf, tau(frm), part)
+        ssem, rsem = spread_sems(buf, base)
+        i = base + k
+        send(b, b, ssem.at[i], rsem.at[i], (m, to))
+
     def spread(buf, base, part=None):
-        b = at_block(buf, me_tau, part)
-        send(b, b, ts.at[base + 4], tr.at[base + 4], (m, ty))
-        for k in (2, 1, 3):
-            send(b, b, ts.at[base + k], tr.at[base + k], (m, along_x(k)))
+        for k, to in ((4, ty), (2, along_x(2)), (1, along_x(1)), (3, along_x(3))):
+            spread_copy(buf, base, part, k, t, to)
 
     def pass_on(buf, base, part=None, to=(2, 1, 3)):
-        b = at_block(buf, tau(ty), part)
-        arrive(b, ts.at[base + 4], tr.at[base + 4], (m, ty))
+        spread_wait(buf, base, 4, part)
         for k in to:
-            send(b, b, ts.at[base + 4 + k], tr.at[base + 4 + k], (m, along_x(k)))
+            spread_copy(buf, base, part, 4 + k, ty, along_x(k))
 
     def pass_back(buf, base, part):
         spread_wait(buf, base, 2, part)
-        b = at_block(buf, tau(along_x(2)), part)
-        send(b, b, ts.at[base + 6], tr.at[base + 6], (m, ty))
+        spread_copy(buf, base, part, 6, along_x(2), ty)
 
     def spread_wait(buf, base, k, part=None):
-        frm = source(k)
-        arrive(at_block(buf, tau(frm), part), ts.at[base + k], tr.at[base + k], (m, frm))
+        ssem, rsem = spread_sems(buf, base)
+        i = base + k
+        arrive(at_block(buf, tau(source(k)), part), ssem.at[i], rsem.at[i], (m, ty))
 
     def ring_send(s):
         for hh in (0, 1):
@@ -192,15 +227,7 @@
                 send(c, c, cs2.at[i], cr2.at[i], c_dev)
 
     def ring_end():
-        for s in range(1, 9):
-            for hh in (0, 1):
-                for sign in (1, -1):
-                    if s == 8 and (hh == 0) != (sign > 0):
-                        continue
-                    i = (sign < 0) * 16 + (s - 1) * 2 + hh
-                    arrive(chunk(gr, -sign * s, hh, sib), cs2.at[i], cr2.at[i], c_dev)
-        for hh in (0, 1):
-            arrive(chunk(gr, 0, hh, sib), cs2.at[32 + hh], cr2.at[32 + hh], c_dev)
+        arrive(gr.at[pl.ds(0, 4)], cs2.at[0], cr2.at[0], c_dev)
 
     def round_of(tile, held, got, ssem, rsem):
         def begin(n, *links):
@@ -209,8 +236,8 @@
                 send(held.at[n], got.at[k], ssem.at[k], rsem.at[k], dev)
 
         def end(*ks):
+            arrive(got.at[pl.ds(ks[0], len(ks))], ssem.at[ks[0]], rsem.at[ks[0]], c_dev)
             for k in ks:
-                arrive(got.at[k], ssem.at[k], rsem.at[k], c_dev)
                 tile[...] += got[k]
 
         return begin, end
@@ -246,8 +273,7 @@
         c = chunk(gr, 0, hh)
         send(c, c, cs2.at[32 + hh], cr2.at[32 + hh], c_dev)
     pass_on(ksa, 0)
-    near_wait(-4)
-    near_wait(4)
+    near_wait(-4, 4)
     near_wait(8)
     mt_add(2, 3, 4)
     mt_send(2, (1, y_dev))
@@ -255,22 +281,14 @@
         send(block(gi, r, half, core), block(gi, r, half, core), cs.at[r], cr.at[r], c_dev)
     ring_wait(1)
     for r in range(4):
-        for o in OFFSETS:
-            if (o - r) % 4 == 0:
-                k = OFFSETS.index(o)
-                arrive(chunk(gi, o, other), ys.at[k], yr.at[k], y_dev)
+        arrive(block(gi, r, other, core), ys.at[r], rr.at[7 + r], y_dev)
         send(block(gi, r, other, core), block(gi, r, other, core), cs.at[4 + r], cr.at[4 + r], c_dev)
     mt_add(1)
     mt_send(3, (0, c_dev))
-    for k in (1, 3, 2):
-        spread_wait(ksa, 0, k)
-        spread_wait(ksa, 0, k + 4)
+    arrive(ksa.at[pl.ds(0, 6)], s_ks.at[0], r_ks.at[0], c_dev)
     for c in loads[6:]:
         c.wait()
-    for r in range(4):
-        arrive(block(gi, r, half, sib), cs.at[r], cr.at[r], c_dev)
-    for r in range(4):
-        arrive(block(gi, r, other, sib), cs.at[4 + r], cr.at[4 + r], c_dev)
+    arrive(gi.at[pl.ds(0, 4)], cs.at[0], cr.at[0], c_dev)
 
     mt_add(0)
     ring_wait(2)
@@ -285,7 +303,7 @@
     def key_copy(k, h):
         tgt = lax.rem(t + k, 8)
         u = pl.ds(h * 160, 160)
-        return copy(bsend.at[k, u], rsb.at[me_tau, u], ts.at[32 + 8 * h + k], tr.at[32 + 8 * h + k], (m, tgt))
+        return copy(bsend.at[k, u], rsb.at[me_tau, u], s_key.at[0], rr.at[17 + h], (m, tgt))
 
     def key_step(i, carry):
         k = 7 - i
@@ -330,10 +348,7 @@
     vd = jnp.zeros((1, 128), F32)
     for h in (0, 1):
         u = pl.ds(h * 160, 160)
-        for k in range(1, 8):
-            frm = lax.rem(t + 8 - k, 8)
-            i = 32 + 8 * h + k
-            arrive(rsb.at[tau(frm), u], ts.at[i], tr.at[i], (m, frm))
+        arrive(rsb.at[pl.ds(0, 7), u], s_key.at[0], rr.at[17 + h], c_dev)
         pre = rsb[0, u].astype(F32)
         for k in range(1, 8):
             pre = pre + rsb[k, u].astype(F32)
@@ -346,24 +361,24 @@
             line = lax.broadcasted_iota(jnp.int32, (16, 128), 0)
             tail = jnp.where(line == 0, vhigh, jnp.where(line == 1, vd - vhigh, 0.0))
             hid[me_tau, 320:336] = tail.astype(BF)
-        spread(hid, 8 + 8 * h, h)
+        spread(hid, 8 * h, h)
         if h == 0:
             ring_wait(4)
-    pass_on(hid, 8, 0, (1, 3))
+    pass_on(hid, 0, 0, (1, 3))
     value_step(0, 0)
     ring_wait(5)
-    pass_on(hid, 16, 1, (1, 3))
-    pass_back(hid, 8, 0)
+    pass_on(hid, 8, 1, (1, 3))
+    pass_back(hid, 0, 0)
     value_step(1, 4)
     y_step(0)
-    pass_back(hid, 16, 1)
+    pass_back(hid, 8, 1)
     value_step(2, 2)
     y_step(1)
 
     def value_loop(p, carry):
         k = 2 * p - 5
-        spread_wait(hid, 8, k, 0)
-        spread_wait(hid, 16, k, 1)
+        spread_wait(hid, 0, k, 0)
+        spread_wait(hid, 8, k, 1)
         value_step(p, k)
         y_step(p - 1)
         return carry
@@ -371,15 +386,15 @@
     lax.fori_loop(3, 5, value_loop, 0)
     ring_wait(6)
     lax.fori_loop(5, 7, value_loop, 0)
-    spread_wait(hid, 8, 6, 0)
-    spread_wait(hid, 16, 6, 1)
+    spread_wait(hid, 0, 6, 0)
+    spread_wait(hid, 8, 6, 1)
     value_step(7, 6)
     y_step(6)
     vd_send(0, (0, c_dev))
     y_step(7)
     vd_add(0)
     vd_send(1, (1, y_dev))
-    spread(vpa, 24)
+    spread(vpa, 0)
     ring_wait(7)
     z_step(0, 0)
     z_step(1, 4)
@@ -413,7 +428,7 @@
             send(src, dst, s_z.at[6 * c + i], r_z.at[6 * c + i], at_z(d))
     vd_add(1)
     vd_send(2, *near_links)
-    pass_on(vpa, 24)
+    pass_on(vpa, 0)
 
     def gathered(dz, w):
         a, b = slot(dz)
@@ -426,8 +441,8 @@
 
     for c in (0, 1):
         w = spans[c]
-        for i, (_, dst, d) in enumerate(near_copies(c)):
-            arrive(dst, s_z.at[6 * c + i], r_z.at[6 * c + i], at_z(-d))
+        arrive(rn.at[:, :, :, w], s_z.at[6 * c], r_z.at[6 * c], c_dev)
+        arrive(rn2.at[:, :, :, w], s_z.at[6 * c], r_z.at[6 * c + 2], c_dev)
         for k in (2, 0, 1):
             total = gathered(FAR[k], w)
             if k < 2:
@@ -443,29 +458,38 @@
 
     for a in range(0, 320, 64):
         ku_ref[a : a + 64] = outer(wgt_k[a : a + 64], gr[:, :, :, :, :, 0:640].reshape(1024, 640))
-    for k in (1, 3, 2):
-        spread_wait(vpa, 24, k)
-        spread_wait(vpa, 24, k + 4)
+    arrive(vpa.at[:, pl.ds(0, 768)], s_vp.at[0], r_vp.at[0], c_dev)
     right = gr[:, :, :, :, :, 640:1280].reshape(1024, 640)
     for a in range(0, 320, 64):
         vu_ref[a : a + 64] = outer(vpa[a : a + 64], right)
 
-    for c in pending:
-        c.wait_send()
-    for k in range(1, 8):
-        for h in (0, 1):
-            key_copy(k, h).wait_send()
-    for b in range(8):
-        copy(psend.at[b], rsib.at[b], s_core.at[b], r_core.at[b], c_dev).wait_send()
-        copy(ysend.at[b], ry.at[b], s_y.at[b], r_y.at[b], y_dev).wait_send()
+    sent(gi.at[pl.ds(0, 7), 0, 0, 0], zs.at[0])
+    sent(gi.at[0], zs.at[7])
+    sent(gi.at[pl.ds(0, 2)], ys.at[0])
+    sent(gi.at[pl.ds(0, 4)], cs.at[0])
+    sent(gr.at[pl.ds(0, 7), :, :, 0], gs.at[0])
+    sent(gr.at[0, 0, :, 0], gs.at[14])
+    sent(gr.at[pl.ds(0, 4)], cs2.at[0])
+    sent(mine_r, ys2)
+    sent(ksa.at[pl.ds(0, 7)], s_ks.at[0])
+    sent(vpa.at[:, pl.ds(0, 896)], s_vp.at[0])
+    for h in (0, 1):
+        sent(hid.at[pl.ds(0, 7), parts[h]], s_hid.at[8 * h])
+    sent(bsend.at[pl.ds(1, 7)], s_key.at[0])
+    sent(psend, s_core.at[0])
+    sent(ysend, s_y.at[0])
+    for c, w in enumerate(spans):
+        sent(zb.at[pl.ds(0, 6), :, :, w], s_z.at[6 * c])
+        sent(fb.at[:, :, w], s_f.at[3 * c])
+    sent(mtr, s_mt.at[0])
+    sent(vdr, s_vd.at[0])
     vd_add(5, 6, 7)
     vd = SIGMA * jnp.sum(jnp.where(spot, vdt[pl.ds(st, 1)], 0.0), axis=1, keepdims=True)
     for c, w in enumerate(spans):
         total = gathered(0, w) + rn2[0, 0, :, w].astype(F32) + rn2[1, 0, :, w].astype(F32)
         total = total + vd * vsv[:, w].astype(F32)
+        arrive(rf.at[:, :, w], s_f.at[3 * c], r_f.at[3 * c], c_dev)
         for k in (0, 1, 2):
-            _, dst, ssem, rsem, dev = far_copy(k, c)
-            arrive(dst, ssem, rsem, dev)
             total = total + rf[k, :, w].astype(F32)
         out_ref[:, w] = total.astype(BF)
 
@@ -523,9 +547,7 @@
             pltpu.VMEM((4, 16, 128), F32),
             pltpu.VMEM((8, 16, 128), F32),
         ]
-        + [dma((n,)) for n in (8, 15, 15, 16, 16, 8, 8, 32, 32)]
-        + [dma(()), dma(())]
-        + [dma((n,)) for n in (34, 34, 48, 48, 8, 8, 8, 8, 12, 12, 6, 6, 8, 8, 8, 8)],
+        + [dma((n,)) for n in (8, 21, 29, 32, 20, 8, 8)],
         compiler_params=pltpu.CompilerParams(
             collective_id=0, has_side_effects=True, vmem_limit_bytes=48 * 2**20
         ),

time: 79.1 us -> 76.6 us (0.968)
  the two profiles are of different devices: /device:TPU:64 before, /device:TPU:32 now
where the time goes in v3:
time: 76.6 us; the launch traced here: 76.5 us
  Pallas kernels  75.8 us (99%)
    pallas_call x1, Pallas kernels, body(): pl.pallas_call(kernel, out_shape=(jax.ShapeDtypeStruct((16, 640), BF), ja...  74.9 us

profile of v3, /device:TPU:32, one launch (start us, length us, event | category | flops | bytes accessed | tf_op | source)
XLA Modules:
  0.0 76.5 jit_solution(13934939891490177408)
XLA Ops:
  0.6 74.9 %step.1 = (bf16[16,640]{1,0:T(8,128)(2,1)S(1)}, bf16[320,640]{1,0:T(8,128)(2,1)S(1)}, bf16[320,640]{1,0:T(8,128)(2,1)S(1)}) custom-call(bf16[16,640]{1,0:T(8,128)(2,1)} %x_ref.1, bf16[320,640]{1,0:T(8,128)(2,1)} %bitcast.5, bf16[320,640]{1,0:T(8,128)(2,1)} %vw_ref.1, bf16[16,640]{1,0:T(8,128)(2,1)} %kp_ref.1, bf16[320,128]{1,0:T(8,128)(2,1)} %bitcast.7, ...), custom_call_target="tpu_custom_call" | custom-call | flops 1700000000 | bytes 4000000 | tf_op jit(solution)/shard_map/step/pallas_call | solution.py:510
  75.5 0.9 %store.1 = (bf16[16,640]{1,0:T(8,128)(2,1)}, bf16[320,640]{1,0:T(8,128)(2,1)}, bf16[320,640]{1,0:T(8,128)(2,1)}) custom-call(bf16[16,640]{1,0:T(8,128)(2,1)S(1)} %get-tuple-element.9.refs_0_, bf16[320,640]{1,0:T(8,128)(2,1)S(1)} %get-tuple-element.10.refs_1_, bf16[320,640]{1,0:T(8,128)(2,1)S(1)} %get-tuple-element.11.refs_2_), custom_call_target="tpu_custom_call" | custom-call | tf_op jit(solution)/shard_map/store/pallas_call | solution.py:558

commit v4 on v3

--- a/solution.py
+++ b/solution.py
@@ -70,10 +70,8 @@
     zs = Shared(ss, lambda k: 0 if k < 7 else 1)
     ys, cs, cs2, s_ks, s_vp, s_key, s_core, s_y, s_mt, s_vd = (Shared(ss, n) for n in range(2, 12))
     gs = Shared(ss, lambda k: 12 if k in (14, 31) else 13)
-    s_hid = Shared(ss, lambda k: 14 + k // 8)
-    s_z = Shared(ss, lambda k: 16 + k // 6)
-    s_f = Shared(ss, lambda k: 18 + k // 3)
-    ys2, yr2 = ss.at[20], rr.at[0]
+    s_z, s_f = Shared(ss, 15), Shared(ss, 16)
+    ys2, yr2 = ss.at[17], rr.at[0]
     zr = Shared(rr, lambda k: 1 + k if k < 3 else 4 if k < 7 else 5 if k < 13 else 6)
     yr = Shared(rr, lambda k: 7 + OFFSETS[k] % 4)
     cr, cr2 = Shared(rr, 11), Shared(rr, 12)
@@ -178,7 +176,7 @@
     def spread_sems(buf, base):
         if buf is ksa:
             return s_ks, r_ks
-        return (s_vp, r_vp) if buf is vpa else (Shared(ss, 14 + base // 8), tr)
+        return (s_vp, r_vp) if buf is vpa else (Shared(ss, 14), tr)
 
     def spread_copy(buf, base, part, k, frm, to):
         b = at_block(buf, tau(frm), part)
@@ -211,19 +209,18 @@
                     continue
                 i = (sign < 0) * 16 + (s - 1) * 2 + hh
                 c = chunk(gr, -sign * (s - 1), hh)
-                send(c, c, gs.at[i], gv.at[i], at_z(sign))
+                send(c, c, gs.at[i], gv.at[(s - 1) * 2 + hh], at_z(sign))
 
     def ring_wait(s):
         for hh in (0, 1):
-            for sign in (1, -1):
-                if s == 8 and (hh == 0) != (sign > 0):
-                    continue
-                i = (sign < 0) * 16 + (s - 1) * 2 + hh
+            signs = (1, -1) if s < 8 else ((1,) if hh == 0 else (-1,))
+            n = (s - 1) * 2 + hh
+            arrive(gr.at[0, 0, pl.ds(0, len(signs)), 0], gs.at[0], gv.at[n], c_dev)
+            for sign in signs:
+                i = (sign < 0) * 16 + n
                 c = chunk(gr, -sign * s, hh)
-                arrive(c, gs.at[i], gv.at[i], at_z(-sign))
                 if s < 7 or (s == 7 and (hh == 0) == (sign > 0)):
-                    n = i + 2
-                    send(c, c, gs.at[n], gv.at[n], at_z(sign))
+                    send(c, c, gs.at[i + 2], gv.at[n + 2], at_z(sign))
                 send(c, c, cs2.at[i], cr2.at[i], c_dev)
 
     def ring_end():
@@ -473,14 +470,12 @@
     sent(mine_r, ys2)
     sent(ksa.at[pl.ds(0, 7)], s_ks.at[0])
     sent(vpa.at[:, pl.ds(0, 896)], s_vp.at[0])
-    for h in (0, 1):
-        sent(hid.at[pl.ds(0, 7), parts[h]], s_hid.at[8 * h])
+    sent(hid.at[pl.ds(0, 7)], ss.at[14])
     sent(bsend.at[pl.ds(1, 7)], s_key.at[0])
     sent(psend, s_core.at[0])
     sent(ysend, s_y.at[0])
-    for c, w in enumerate(spans):
-        sent(zb.at[pl.ds(0, 6), :, :, w], s_z.at[6 * c])
-        sent(fb.at[:, :, w], s_f.at[3 * c])
+    sent(zb.at[pl.ds(0, 6)], s_z.at[0])
+    sent(fb, s_f.at[0])
     sent(mtr, s_mt.at[0])
     sent(vdr, s_vd.at[0])
     vd_add(5, 6, 7)
@@ -547,7 +542,7 @@
             pltpu.VMEM((4, 16, 128), F32),
             pltpu.VMEM((8, 16, 128), F32),
         ]
-        + [dma((n,)) for n in (8, 21, 29, 32, 20, 8, 8)],
+        + [dma((n,)) for n in (8, 18, 29, 16, 20, 8, 8)],
         compiler_params=pltpu.CompilerParams(
             collective_id=0, has_side_effects=True, vmem_limit_bytes=48 * 2**20
         ),

time: 76.6 us -> 76.6 us (level)
  the two profiles are of different devices: /device:TPU:32 before, /device:TPU:36 now
where the time goes in v4:
time: 76.6 us; the launch traced here: 76.5 us
  Pallas kernels  75.9 us (99%)
    pallas_call x1, Pallas kernels, body(): pl.pallas_call(kernel, out_shape=(jax.ShapeDtypeStruct((16, 640), BF), ja...  74.9 us

profile of v4, /device:TPU:36, one launch (start us, length us, event | category | flops | bytes accessed | tf_op | source)
XLA Modules:
  0.0 76.5 jit_solution(18249270798670171048)
XLA Ops:
  0.6 74.9 %step.1 = (bf16[16,640]{1,0:T(8,128)(2,1)S(1)}, bf16[320,640]{1,0:T(8,128)(2,1)S(1)}, bf16[320,640]{1,0:T(8,128)(2,1)S(1)}) custom-call(bf16[16,640]{1,0:T(8,128)(2,1)} %x_ref.1, bf16[320,640]{1,0:T(8,128)(2,1)} %bitcast.5, bf16[320,640]{1,0:T(8,128)(2,1)} %vw_ref.1, bf16[16,640]{1,0:T(8,128)(2,1)} %kp_ref.1, bf16[320,128]{1,0:T(8,128)(2,1)} %bitcast.7, ...), custom_call_target="tpu_custom_call" | custom-call | flops 1700000000 | bytes 4000000 | tf_op jit(solution)/shard_map/step/pallas_call | solution.py:505
  75.6 0.9 %store.1 = (bf16[16,640]{1,0:T(8,128)(2,1)}, bf16[320,640]{1,0:T(8,128)(2,1)}, bf16[320,640]{1,0:T(8,128)(2,1)}) custom-call(bf16[16,640]{1,0:T(8,128)(2,1)S(1)} %get-tuple-element.9.refs_0_, bf16[320,640]{1,0:T(8,128)(2,1)S(1)} %get-tuple-element.10.refs_1_, bf16[320,640]{1,0:T(8,128)(2,1)S(1)} %get-tuple-element.11.refs_2_), custom_call_target="tpu_custom_call" | custom-call | tf_op jit(solution)/shard_map/store/pallas_call | solution.py:553
